TPU v7x, 32 devices: a whole 2x2x4 slice. The times are simulated.
32 devices in a mesh: row: 16 (over z, y, core), col: 2 (over x).
Axes of the slice: x: 2, y: 2, z: 4, core: 2. Of those that a mesh axis runs over, the one named last changes fastest.
Arguments:
- known_inverse: float32 [20480, 20480], P('row', 'col'), may hold values from -1.7818667 to 1.7818667, as said below
- first_panel: float32 [20480, 512], P('col', 'row'), may hold values from -1.25 to 1.25
- second_panel: float32 [20480, 512], P('col', 'row'), may hold values from -1.25 to 1.25
- coupling: float32 [512, 512], replicated, may hold values from -0.25 to 0.25
- first_diag: float32 [512, 512], replicated, may hold values from -6 to 6
- second_diag: float32 [512, 512], replicated, may hold values from -6 to 6
- first_present: int32 [160], replicated, may hold values 0 or 1
- second_present: int32 [160], replicated, may hold values 0 or 1
Outputs:
- first_block: float32 [20480, 512], P(('row', 'col'))
- first_inverse_diag: float32 [512, 512], P(None, 'col')
- second_block: float32 [20480, 512], P(('row', 'col'))
- second_cross: float32 [512, 512], P(None, 'col')
- second_inverse_diag: float32 [512, 512], P(None, 'col')
Inputs may be any that keep to these rules, and one draw needn't show every extreme that they name: known_inverse is exactly symmetric.
All inputs are finite; a program needn't handle non-finite values.
Results may differ from a plain program's by a relative error of at most 0.000098.
Values sent between devices are 32-bit elements; how exact they have to be, the bound alone decides.
No kernel may reach another device: no remote copies, remote signals or barrier semaphores. Data moves between devices by JAX's collectives and lax.ppermute only.
A program may use at most 192 MiB of HBM per device.

v0:
```python
import jax
import jax.numpy as jnp
from jax import lax
from jax.sharding import PartitionSpec as P

BLK = 128


def product(left, right):
    return jnp.dot(left, right, precision=lax.Precision.HIGHEST, preferred_element_type=jnp.float32)


def transposed(left, right):
    return lax.dot_general(
        left,
        right,
        (((0,), (0,)), ((), ())),
        precision=lax.Precision.HIGHEST,
        preferred_element_type=jnp.float32,
    )


def masked(panel, present, col_index):
    row_total, col_total = panel.shape
    blocks = row_total // BLK
    local = lax.dynamic_slice_in_dim(present, col_index * blocks, blocks)
    shaped = panel.reshape(blocks, BLK, col_total) * local.astype(jnp.float32)[:, None, None]
    return shaped.reshape(row_total, col_total)


def piece_products(known_inverse, column_one, column_two, piece_one, piece_two, coupling):
    first_block = -lax.psum_scatter(
        product(known_inverse, column_one), "col", scatter_dimension=0, tiled=True
    )
    reached = lax.psum_scatter(
        product(known_inverse, column_two), "col", scatter_dimension=0, tiled=True
    )
    first_partial = transposed(piece_one, first_block)
    second_block = -(reached + product(first_block, coupling))
    cross_partial = transposed(first_block, piece_two)
    diag_partial = transposed(piece_two, second_block)
    return (first_block, second_block, first_partial, cross_partial, diag_partial)


def on_device(
    known_inverse,
    first_panel,
    second_panel,
    coupling,
    first_diag,
    second_diag,
    first_present,
    second_present,
):
    col_count = lax.axis_size("col")
    row_index = lax.axis_index("row")
    col_index = lax.axis_index("col")
    local_one = masked(first_panel, first_present, col_index)
    local_two = masked(second_panel, second_present, col_index)
    column_one, column_two = (
        lax.all_gather(local_one, "row", axis=1, tiled=True),
        lax.all_gather(local_two, "row", axis=1, tiled=True),
    )
    band_rows = known_inverse.shape[0]
    block_cols = known_inverse.shape[1]
    width_total = coupling.shape[0]
    owner = row_index * band_rows // block_cols
    offset = row_index * band_rows % block_cols
    is_owner = (col_index == owner).astype(jnp.float32)
    band_one = lax.dynamic_slice_in_dim(column_one, offset, band_rows) * is_owner
    band_two = lax.dynamic_slice_in_dim(column_two, offset, band_rows) * is_owner
    piece_one, piece_two = (
        lax.psum_scatter(band_one, "col", scatter_dimension=0, tiled=True),
        lax.psum_scatter(band_two, "col", scatter_dimension=0, tiled=True),
    )
    first_block, second_block, first_partial, cross_partial, diag_partial = piece_products(
        known_inverse, column_one, column_two, piece_one, piece_two, coupling
    )
    col_width = width_total // col_count
    col_start = col_index * col_width
    first_sum = lax.psum(first_partial, ("row", "col"))
    first_inverse_diag = first_diag - first_sum
    cross_sum, diag_sum = lax.psum((cross_partial, diag_partial), ("row", "col"))
    second_cross = -(cross_sum + product(first_inverse_diag, coupling))
    second_inverse_diag = second_diag - diag_sum - transposed(coupling, second_cross)
    first_out = lax.dynamic_slice_in_dim(first_inverse_diag, col_start, col_width, 1)
    cross_out = lax.dynamic_slice_in_dim(second_cross, col_start, col_width, 1)
    second_out = lax.dynamic_slice_in_dim(second_inverse_diag, col_start, col_width, 1)
    return (first_block, first_out, second_block, cross_out, second_out)


def solution(mesh):
    in_specs = (P("row", "col"), P("col", "row"), P("col", "row"), P(), P(), P(), P(), P())
    out_specs = (
        P(("row", "col"), None),
        P(None, "col"),
        P(("row", "col"), None),
        P(None, "col"),
        P(None, "col"),
    )
    return jax.shard_map(
        on_device, mesh=mesh, in_specs=in_specs, out_specs=out_specs, check_vma=False
    )
```

profile of v0, /device:TPU:0, one launch (start us, length us, event | category | flops | bytes accessed | tf_op | source)
XLA Modules:
  0.0 556.2 jit_solution(14909715024471584031)
XLA Ops:
  7.2 0.0 copy-start
  7.2 0.0 all-gather.3.cloned.1.call-start
  7.2 0.9 dynamic-slice_convert_fusion
  8.1 0.1 broadcast_bitcast_fusion.1
  8.2 2.5 broadcast_multiply_fusion.1
  10.6 0.0 copy-start.4
  10.6 0.0 all-gather.3.cloned.1.call-update
  10.7 0.0 all-gather.5.cloned.1.call-start
  10.7 0.1 broadcast_bitcast_fusion
  10.8 1.2 copy-done.4
  12.0 1.2 broadcast_multiply_fusion
  13.1 0.0 all-gather.5.cloned.1.call-update
  13.1 0.0 reduce-scatter.5.cloned.1.call-start
  13.2 109.2 %all-gather.3.cloned.1.call-done = f32[10240,512]{0,1:T(8,128)} async-done(((f32[10240,32]{0,1:T(8,128)}), f32[10240,512]{0,1:T(8,128)}) %all-gather.3.cloned.1.call-update) | async-done | bytes 20971536 | tf_op jit(solution)/shard_map/all_gather | solution.py:61
  122.4 90.1 %convolution_bitcast_fusion.1 = f32[1280,512]{0,1:T(8,128)} fusion(f32[10240,512]{0,1:T(8,128)} %all-gather.3.cloned.1.call-done, f32[1280,10240]{1,0:T(8,128)} %param.8), kind=kOutput, calls=%fused_computation.1 | convolution fusion | flops 80530636800 | bytes 76021760 | tf_op jit(solution)/shard_map/dot_general | solution.py:10
  212.5 0.0 reduce-scatter.5.cloned.1.call-update
  212.5 0.0 reduce-scatter.7.cloned.1.call-start
  212.6 4.2 dynamic-slice_multiply_fusion.1
  216.8 0.0 reduce-scatter.7.cloned.1.call-update
  216.8 0.0 reduce-scatter.11.cloned.1.call-start
  216.9 16.5 %all-gather.5.cloned.1.call-done = f32[10240,512]{0,1:T(8,128)} async-done(((f32[10240,32]{0,1:T(8,128)}), f32[10240,512]{0,1:T(8,128)}) %all-gather.5.cloned.1.call-update) | async-done | bytes 20971536 | tf_op jit(solution)/shard_map/all_gather | solution.py:62
  233.4 4.1 dynamic-slice_multiply_fusion
  237.5 0.0 reduce-scatter.11.cloned.1.call-update
  237.5 0.2 reduce-scatter.9.cloned.1.call-start
  237.7 90.1 %convolution_bitcast_fusion = f32[1280,512]{0,1:T(8,128)} fusion(f32[10240,512]{0,1:T(8,128)} %all-gather.5.cloned.1.call-done, f32[1280,10240]{1,0:T(8,128)} %param.8), kind=kOutput, calls=%fused_computation | convolution fusion | flops 80530636800 | bytes 76021760 | tf_op jit(solution)/shard_map/dot_general | solution.py:10
  327.9 0.0 reduce-scatter.9.cloned.1.call-update
  327.9 0.3 all-reduce.3.cloned.1.call-start
  328.2 0.0 reduce-scatter.5.cloned.1.call-done
  328.2 0.0 copy-start.1
  328.2 0.0 reduce-scatter.7.cloned.1.call-done
  328.2 5.4 fusion.5
  333.7 19.1 %reduce-scatter.11.cloned.1.call-done = f32[640,512]{0,1:T(8,128)} async-done(((f32[1280,512]{0,1:T(8,128)}), f32[640,512]{0,1:T(8,128)}) %reduce-scatter.11.cloned.1.call-update) | async-done | bytes 1310736 | tf_op jit(solution)/shard_map/reduce_scatter | solution.py:74
  352.8 0.0 copy-done.1
  352.8 4.9 fusion.2
  357.7 34.9 %reduce-scatter.9.cloned.1.call-done = f32[640,512]{0,1:T(8,128)} async-done(((f32[1280,512]{0,1:T(8,128)}), f32[640,512]{0,1:T(8,128)}) %reduce-scatter.9.cloned.1.call-update) | async-done | bytes 1310736 | tf_op jit(solution)/shard_map/reduce_scatter | solution.py:35
  392.6 0.0 copy-done
  392.6 0.0 copy-start.3
  392.6 4.3 fusion
  396.9 0.0 copy-start.2
  396.9 1.0 copy-done.2
  398.0 0.0 copy-done.3
  398.0 3.6 fusion.7
  401.6 0.0 all-reduce.3.cloned.1.call-update
  401.6 2.8 copy.16
  404.4 1.2 neg.9
  405.6 0.0 copy-start.5
  405.6 2.9 copy.15
  408.5 132.1 %all-reduce.3.cloned.1.call-done = (f32[512,512]{1,0:T(8,128)}, f32[512,512]{1,0:T(8,128)}, f32[512,512]{1,0:T(8,128)}) async-done(((f32[512,512]{1,0:T(8,128)}, f32[512,512]{1,0:T(8,128)}, f32[512,512]{1,0:T(8,128)}), (f32[512,512]{1,0:T(8,128)}, f32[512,512]{1,0:T(8,128)}, f32[512,512]{1,0:T(8,128)})) %all-reduce.3.cloned.1.call-update) | async-done | bytes 3145744 | tf_op jit(solution)/shard_map/psum | solution.py:81
  540.6 0.0 copy-done.5
  540.6 1.4 sub.14
  542.0 0.0 copy-start.6
  542.1 0.8 constant_dynamic-slice_fusion.1
  542.9 0.6 copy-done.6
  543.5 2.1 fusion.1
  545.6 0.8 constant_dynamic-slice_fusion
  546.4 0.0 copy-start.7
  546.4 0.0 copy-start.8
  546.4 1.9 convolution_bitcast_fusion.2
  548.3 0.0 copy-done.7
  548.3 0.0 copy-done.8
  548.3 1.0 dynamic-slice_subtract_fusion
Async XLA Ops:
  7.2 385.4 %copy-start = (f32[512,512]{1,0:T(8,128)S(1)}, f32[512,512]{1,0:T(8,128)}, u32[]{:S(2)}) copy-start(f32[512,512]{1,0:T(8,128)} %param.11) | copy-start | bytes 3145732
  7.2 115.2 %all-gather.3.cloned.1.call-start = ((), (), s32[]{:S(2)}) async-start(), calls=%async_computation.4 | async-start | bytes 22282240 | tf_op jit(solution)/shard_map/all_gather | solution.py:61
  10.6 1.3 copy-start.4
  10.7 222.7 %all-gather.5.cloned.1.call-start = ((), (), s32[]{:S(2)}) async-start(), calls=%async_computation.7 | async-start | bytes 22282240 | tf_op jit(solution)/shard_map/all_gather | solution.py:62
  13.1 315.1 %reduce-scatter.5.cloned.1.call-start = ((), (), s32[]{:S(2)}) async-start(), calls=%async_computation.5 | async-start | bytes 3932160 | tf_op jit(solution)/shard_map/reduce_scatter | solution.py:32
  212.5 115.7 %reduce-scatter.7.cloned.1.call-start = ((), (), s32[]{:S(2)}) async-start(), calls=%async_computation.6 | async-start | bytes 3932160 | tf_op jit(solution)/shard_map/reduce_scatter | solution.py:73
  216.8 135.9 %reduce-scatter.11.cloned.1.call-start = ((), (), s32[]{:S(2)}) async-start(), calls=%async_computation.9 | async-start | bytes 3932160 | tf_op jit(solution)/shard_map/reduce_scatter | solution.py:74
  237.5 155.1 %reduce-scatter.9.cloned.1.call-start = ((), (), s32[]{:S(2)}) async-start(), calls=%async_computation.8 | async-start | bytes 3932160 | tf_op jit(solution)/shard_map/reduce_scatter | solution.py:35
  327.9 212.7 %all-reduce.3.cloned.1.call-start = ((), (), s32[]{:S(2)}) async-start(), calls=%async_computation.10 | async-start | bytes 6291456 | tf_op jit(solution)/shard_map/psum | solution.py:81
  328.2 24.6 %copy-start.1 = (f32[640,512]{0,1:T(8,128)S(1)}, f32[640,512]{0,1:T(8,128)}, u32[]{:S(2)}) copy-start(f32[640,512]{0,1:T(8,128)} %reduce-scatter.5.cloned.1.call-done) | copy-start | bytes 3932164
  392.6 5.4 copy-start.3
  396.9 1.1 copy-start.2
  405.6 135.0 %copy-start.5 = (f32[512,512]{1,0:T(8,128)S(1)}, f32[512,512]{1,0:T(8,128)}, u32[]{:S(2)}) copy-start(f32[512,512]{1,0:T(8,128)} %param.12) | copy-start | bytes 3145732
  542.0 1.4 copy-start.6
  546.4 1.9 copy-start.7
  546.4 1.9 copy-start.8
Sparse Core Ops, SparseCore 0:
  10.8 111.5 all-gather.2
  124.5 108.8 all-gather.4
  235.6 37.5 reduce-scatter.4
  275.4 37.5 reduce-scatter.6
  315.1 37.5 reduce-scatter.10
  354.9 37.5 reduce-scatter.8
  401.8 138.8 all-reduce.2
where the time goes:
time: 557 us; the launch traced here: 556 us
  waiting for transfers between devices  312 us (56%)
  matrix products  203 us (36%)
  other arithmetic  16.4 us (3%)
  between operations  14.3 us (3%)
  local copies, waits for them, and re-layouts  10.3 us (2%)
    dot_general x4, matrix products, product(): jnp.dot(left, right, precision=lax.Precision.HIGHEST, preferred_element_t...  187 us
    psum x1, waiting for transfers between devices, on_device(): first_sum = lax.psum(first_partial, ('row', 'col'))  132 us
    all_gather x1, waiting for transfers between devices, on_device(): lax.all_gather(local_one, 'row', axis=1, tiled=True)  109 us
    reduce_scatter x1, waiting for transfers between devices, piece_products(): lax.psum_scatter(product(known_inverse, column_two), 'col', scatter_dimen...  34.9 us
    reduce_scatter x1, waiting for transfers between devices, on_device(): lax.psum_scatter(band_two, 'col', scatter_dimension=0, tiled=True)  19.1 us
    all_gather x1, waiting for transfers between devices, on_device(): lax.all_gather(local_two, 'row', axis=1, tiled=True)  16.5 us
    dot_general x4, matrix products, transposed(): lax.dot_general(left, right, (((0,), (0,)), ((), ())), precision=lax.Prec...  15.9 us
  transfers between devices with their start and end apart: 7, of which 5 were waited for; matrix products, arithmetic and copies ran while one was open for 37% of the time, Pallas kernels for 0%

commit v1 on v0

--- a/solution.py
+++ b/solution.py
@@ -1,9 +1,18 @@
+import functools
+
 import jax
 import jax.numpy as jnp
 from jax import lax
+from jax.experimental import pallas as pl
+from jax.experimental.pallas import tpu as pltpu
 from jax.sharding import PartitionSpec as P
 
 BLK = 128
+GROUP = 4
+SLOTS = 3
+VMEM_BYTES = 50 * 2**20
+LEVELS = (0.55, 0.6, 1.0)
+BF16 = jnp.bfloat16
 
 
 def product(left, right):
@@ -42,7 +51,7 @@
     return (first_block, second_block, first_partial, cross_partial, diag_partial)
 
 
-def on_device(
+def dense(
     known_inverse,
     first_panel,
     second_panel,
@@ -89,6 +98,471 @@
     return (first_block, first_out, second_block, cross_out, second_out)
 
 
+def near(left, right, dims=(((1,), (0,)), ((), ()))):
+    return lax.dot_general(left, right, dims, precision=lax.Precision.HIGH, preferred_element_type=jnp.float32)
+
+
+def in_smem():
+    return pl.BlockSpec(memory_space=pltpu.SMEM)
+
+
+def in_vmem():
+    return pl.BlockSpec(memory_space=pltpu.VMEM)
+
+
+def lanes(start):
+    return pl.ds(pl.multiple_of(start * BLK, BLK), BLK)
+
+
+def split(value):
+    high = value.astype(BF16)
+    return high, (value - high.astype(jnp.float32)).astype(BF16)
+
+
+def present_rows(one, two, panel_one, panel_two, capacity):
+    width, total = panel_one.shape
+    blocks = total // BLK
+
+    def kernel(one_ref, two_ref, first_ref, second_ref, out_ref, list_ref, at_one, at_two, by_one, by_two, size_ref):
+        def body(block, carry):
+            place, size = carry
+            for present_ref, source, at_ref, by_ref in (
+                (one_ref, first_ref, at_one, by_one),
+                (two_ref, second_ref, at_two, by_two),
+            ):
+                here = present_ref[block]
+                spot = jnp.where(here > 0, place, -1)
+                at_ref[size] = spot
+                by_ref[block] = spot
+
+                @pl.when(jnp.logical_and(here > 0, place < capacity))
+                def _(place=place, source=source):
+                    out_ref[:, lanes(place)] = source[:, lanes(block)]
+
+                place = place + here
+            list_ref[size] = block
+            return place, size + jnp.maximum(one_ref[block], two_ref[block])
+
+        place, size = lax.fori_loop(0, blocks, body, (jnp.int32(0), jnp.int32(0)))
+        size_ref[0] = size
+
+        def rest(entry, _):
+            list_ref[entry] = 0
+            at_one[entry] = -1
+            at_two[entry] = -1
+            return 0
+
+        lax.fori_loop(size, blocks, rest, 0)
+
+        def clear(entry, _):
+            out_ref[:, lanes(entry)] = jnp.zeros((width, BLK), jnp.float32)
+            return 0
+
+        lax.fori_loop(jnp.minimum(place, capacity), capacity, clear, 0)
+
+    ints = jax.ShapeDtypeStruct((blocks,), jnp.int32)
+    return pl.pallas_call(
+        kernel,
+        in_specs=[in_smem(), in_smem(), in_vmem(), in_vmem()],
+        out_specs=[in_vmem()] + [in_smem()] * 6,
+        out_shape=[
+            jax.ShapeDtypeStruct((width, capacity * BLK), jnp.float32),
+            ints,
+            ints,
+            ints,
+            ints,
+            ints,
+            jax.ShapeDtypeStruct((1,), jnp.int32),
+        ],
+        compiler_params=pltpu.CompilerParams(vmem_limit_bytes=VMEM_BYTES),
+        cost_estimate=pl.CostEstimate(flops=0, transcendentals=0, bytes_accessed=20 * 2**20),
+        name="present_rows",
+    )(one, two, panel_one, panel_two)
+
+
+def panel_product(known_inverse, sources, places, band, side, whole):
+    block_list, at_one, at_two, by_one, by_two, size = places
+    rows, total = known_inverse.shape
+    half = rows // 2
+    shares = 2 if whole else 1
+    widths = [source.shape[0] for source in sources]
+    width = sum(widths)
+    starts = [sum(widths[:i]) for i in range(len(widths))]
+    depth = GROUP * BLK
+    count = len(sources)
+    outs = 2 * shares if whole else 3
+
+    def kernel(where_ref, size_ref, list_ref, one_ref, two_ref, by_one_ref, by_two_ref, known_ref, *refs):
+        source_any, out_refs = refs[:count], refs[count : count + outs]
+        source_refs = refs[count + outs : 2 * count + outs]
+        slots, right, fetched, arrived = refs[2 * count + outs :]
+        products, pieces = out_refs[:shares], out_refs[shares:]
+        steps = (size_ref[0] + GROUP - 1) // GROUP
+        parts = (1 - where_ref[0], where_ref[0])
+
+        def fetch(step, slot):
+            return [
+                pltpu.make_async_copy(
+                    known_ref.at[pl.ds(pl.multiple_of(parts[p] * half, half), half), lanes(list_ref[step * GROUP + g])],
+                    slots.at[slot, p * half : (p + 1) * half, g * BLK : (g + 1) * BLK],
+                    fetched.at[slot, p, g],
+                )
+                for g in range(GROUP)
+                for p in range(shares)
+            ]
+
+        for ahead in range(SLOTS - 1):
+
+            @pl.when(ahead < steps)
+            def _(ahead=ahead):
+                for copy in fetch(ahead, ahead):
+                    copy.start()
+
+        moves = [pltpu.make_async_copy(source_any[i], source_refs[i], arrived.at[i]) for i in range(count)]
+        for move in moves:
+            move.start()
+        for product in products:
+            product[...] = jnp.zeros_like(product)
+        for move in moves:
+            move.wait()
+
+        for p, piece in enumerate(pieces):
+            for panel, by_ref in enumerate((by_one_ref, by_two_ref)):
+                for block in range(half // BLK):
+                    spot = by_ref[where_ref[1] + parts[p] * (half // BLK) + block]
+                    for source, start, height in zip(source_refs, starts, widths):
+                        row = panel * width + start
+                        value = source[:, lanes(jnp.maximum(spot, 0))]
+                        piece[row : row + height, block * BLK : (block + 1) * BLK] = jnp.where(
+                            spot >= 0, value, 0.0
+                        )
+
+        def times(left, other):
+            return lax.dot_general(left, other, (((1,), (1,)), ((), ())), preferred_element_type=jnp.float32)
+
+        def body(step, _):
+            slot = lax.rem(step, SLOTS)
+            later = step + SLOTS - 1
+
+            @pl.when(later < steps)
+            def _():
+                for copy in fetch(later, lax.rem(later, SLOTS)):
+                    copy.start()
+
+            for g in range(GROUP):
+                entry = step * GROUP + g
+                for panel, at_ref in enumerate((one_ref, two_ref)):
+                    spot = at_ref[entry]
+                    keep = jnp.logical_and(spot >= 0, entry < size_ref[0])
+                    for source, start, height in zip(source_refs, starts, widths):
+                        row = panel * width + start
+                        value = source[:, lanes(jnp.maximum(spot, 0))]
+                        high, low = split(jnp.where(keep, value, 0.0))
+                        right[row : row + height, g * BLK : (g + 1) * BLK] = high
+                        right[2 * width + row : 2 * width + row + height, g * BLK : (g + 1) * BLK] = low
+            for copy in fetch(step, slot):
+                copy.wait()
+            high, low = split(slots[slot])
+            both = times(high, right[...])
+            both = both[:, : 2 * width] + both[:, 2 * width :] + times(low, right[: 2 * width, :])
+            for p, product in enumerate(products):
+                product[...] += both[p * half : (p + 1) * half]
+            return 0
+
+        lax.fori_loop(0, steps, body, 0)
+
+    anywhere = pl.BlockSpec(memory_space=pl.ANY)
+    product = jax.ShapeDtypeStruct((half, 2 * width), jnp.float32)
+    piece = jax.ShapeDtypeStruct((2 * width, half), jnp.float32)
+    where = jnp.stack([side, band]).astype(jnp.int32)
+    return pl.pallas_call(
+        kernel,
+        in_specs=[in_smem()] * 7 + [anywhere] * (1 + count),
+        out_specs=[in_vmem()] * outs,
+        out_shape=[product] * shares + [piece] * 2,
+        scratch_shapes=[pltpu.VMEM(source.shape, jnp.float32) for source in sources]
+        + [
+            pltpu.VMEM((SLOTS, shares * half, depth), jnp.float32),
+            pltpu.VMEM((4 * width, depth), BF16),
+            pltpu.SemaphoreType.DMA((SLOTS, shares, GROUP)),
+            pltpu.SemaphoreType.DMA((count,)),
+        ],
+        compiler_params=pltpu.CompilerParams(vmem_limit_bytes=VMEM_BYTES),
+        cost_estimate=pl.CostEstimate(
+            flops=3 * shares * half * total * width * 2 * 2,
+            transcendentals=0,
+            bytes_accessed=shares * half * total * 3,
+        ),
+        name="panel_product",
+    )(where, size, block_list, at_one, at_two, by_one, by_two, known_inverse, *sources)
+
+
+def fold(groups, matrix, before):
+    arrays, firsts, heights = [], [], []
+    for mine, arrived, sources in groups:
+        arrays += [mine, arrived]
+        firsts += [first for _, first in sources]
+        heights.append([array.shape[0] for array, _ in sources])
+    rows = arrays[0].shape[0]
+    total = matrix.shape[0] // 2
+    count = len(arrays)
+    has = before is not None
+
+    def kernel(first_ref, *refs):
+        ins, matrix_ref, out_ref = refs[:count], refs[count], refs[-1]
+
+        def times(left, other):
+            return lax.dot_general(left, other, (((1,), (0,)), ((), ())), preferred_element_type=jnp.float32)
+
+        value = refs[count + 1][...] if has else None
+        entry = 0
+        for index, widths in enumerate(heights):
+            parts = [
+                matrix_ref[pl.ds(pl.multiple_of(panel * total + first_ref[entry + i], 32), w), :]
+                for panel in range(2)
+                for i, w in enumerate(widths)
+            ]
+            entry += len(widths)
+            big, small = split(jnp.concatenate(parts, axis=0))
+            high, low = split(ins[2 * index][...] + ins[2 * index + 1][...])
+            part = times(high, big) + times(high, small) + times(low, big)
+            value = part if value is None else value + part
+        out_ref[...] = value
+
+    return pl.pallas_call(
+        kernel,
+        in_specs=[in_smem()] + [in_vmem()] * (count + 1 + has),
+        out_specs=in_vmem(),
+        out_shape=jax.ShapeDtypeStruct((rows, 2 * total), jnp.float32),
+        compiler_params=pltpu.CompilerParams(vmem_limit_bytes=VMEM_BYTES),
+        cost_estimate=pl.CostEstimate(
+            flops=6 * rows * 2 * total * sum(a.shape[1] for a in arrays[::2]),
+            transcendentals=0,
+            bytes_accessed=8 * rows * total * 2,
+        ),
+        name="fold",
+    )(jnp.stack(firsts).astype(jnp.int32), *arrays, matrix, *([before] if has else []))
+
+
+def own_rows(pieces, is_owner, total):
+    arrays, firsts, heights = [], [], []
+    for own, arrived, sources in pieces:
+        arrays += [own, arrived]
+        firsts += [first for _, first in sources]
+        heights.append([array.shape[0] for array, _ in sources])
+    count = len(arrays)
+    length = arrays[0].shape[1]
+
+    def kernel(first_ref, *refs):
+        ins, outs = refs[:count], refs[count:]
+        entry = 0
+        for index, widths in enumerate(heights):
+            here, there = ins[2 * index], ins[2 * index + 1]
+            row = 0
+            for panel, out in enumerate(outs):
+                for i, w in enumerate(widths):
+                    value = jnp.where(first_ref[0] > 0, here[row : row + w, :], there[row : row + w, :])
+                    out[pl.ds(pl.multiple_of(first_ref[1 + entry + i], 32), w), :] = value
+                    row += w
+            entry += len(widths)
+
+    return pl.pallas_call(
+        kernel,
+        in_specs=[in_smem()] + [in_vmem()] * count,
+        out_specs=[in_vmem()] * 2,
+        out_shape=[jax.ShapeDtypeStruct((total, length), jnp.float32)] * 2,
+        compiler_params=pltpu.CompilerParams(vmem_limit_bytes=VMEM_BYTES),
+        cost_estimate=pl.CostEstimate(flops=0, transcendentals=0, bytes_accessed=12 * total * length),
+        name="own_rows",
+    )(jnp.stack([is_owner] + firsts).astype(jnp.int32), *arrays)
+
+
+def pairs(count, bit):
+    return [(i, i ^ bit) for i in range(count)]
+
+
+def halves(value, dim, side):
+    size = value.shape[dim] // 2
+    return (
+        lax.dynamic_slice_in_dim(value, side * size, size, dim),
+        lax.dynamic_slice_in_dim(value, (1 - side) * size, size, dim),
+    )
+
+
+def summed(value, stages):
+    kept = []
+    for axis, bit in stages:
+        count = lax.axis_size(axis)
+        side = lax.axis_index(axis) // bit % 2
+        mine, theirs = halves(value, 1 if axis == "col" else 0, side)
+        value = mine + lax.ppermute(theirs, axis, pairs(count, bit))
+        if axis == "row":
+            kept.append((bit, side))
+    for bit, side in reversed(kept):
+        other = lax.ppermute(value, "row", pairs(lax.axis_size("row"), bit))
+        value = jnp.where(
+            side == 0, jnp.concatenate([value, other], axis=0), jnp.concatenate([other, value], axis=0)
+        )
+    return value
+
+
+def ring_chip(position, chips):
+    half = chips // 2
+    return jnp.where(position < half, 2 * position, 2 * (chips - 1 - position) + 1)
+
+
+def sparse(
+    known_inverse,
+    first_panel,
+    second_panel,
+    coupling,
+    first_diag,
+    second_diag,
+    first_present,
+    second_present,
+    capacity,
+):
+    rows = lax.axis_size("row")
+    row_index = lax.axis_index("row")
+    col_index = lax.axis_index("col")
+    band_rows, block_cols = known_inverse.shape
+    width = first_panel.shape[1]
+    total = coupling.shape[0]
+    part_rows = band_rows // 2
+    blocks = block_cols // BLK
+    chips = rows // 2
+    reach = chips // 2
+    core = row_index % 2
+    chip = row_index // 2
+    position = jnp.where(chip % 2 == 0, chip // 2, chips - 1 - chip // 2)
+    order = [2 * p for p in range(reach)] + [2 * p + 1 for p in reversed(range(reach))]
+
+    own, block_list, at_one, at_two, by_one, by_two, size = present_rows(
+        lax.dynamic_slice_in_dim(first_present, col_index * blocks, blocks),
+        lax.dynamic_slice_in_dim(second_present, col_index * blocks, blocks),
+        first_panel.T,
+        second_panel.T,
+        capacity,
+    )
+    places = (block_list, at_one, at_two, by_one, by_two, size)
+    owner = row_index * band_rows // block_cols
+    band = row_index * band_rows % block_cols // BLK
+    to_other = []
+    for r in range(rows):
+        o = r * band_rows // block_cols
+        to_other.append((2 * r + o, 2 * r + 1 - o))
+    ring = []
+    for p in range(chips):
+        ring.append((2 * order[p], 2 * order[(p + 1) % chips]))
+        ring.append((2 * order[p] + 1, 2 * order[(p - 1) % chips] + 1))
+
+    def swap(value):
+        return lax.ppermute(value, "row", pairs(rows, 1))
+
+    def start(distance):
+        return 2 * width * ring_chip((position + distance) % chips, chips)
+
+    identity = jnp.eye(total, dtype=jnp.float32)
+    matrix = jnp.concatenate(
+        [
+            jnp.concatenate([-identity, coupling], axis=1),
+            jnp.concatenate([jnp.zeros_like(identity), -identity], axis=1),
+        ],
+        axis=0,
+    )
+
+    other = swap(own)
+    moving = jnp.where(core == 0, jnp.concatenate([own, other]), jnp.concatenate([other, own]))
+    way = jnp.where(core == 0, -1, 1)
+    products, pieces = [], []
+    for distance in range(reach + 1):
+        last = distance == reach
+        if distance == 0:
+            sources = [(moving, start(0))]
+        elif last:
+            shift = jnp.where(core == 0, 0, width)
+            sources = [(moving, start(distance) + shift), (swap(moving), start(distance) + width - shift)]
+        else:
+            sources = [(moving, start(way * distance)), (swap(moving), start(-way * distance))]
+        if not last:
+            if distance + 1 == reach:
+                moving = jnp.where(core == 0, moving[:width], moving[width:])
+            moving = lax.ppermute(moving, "row", ring)
+        arrays = [array for array, _ in sources]
+        if last:
+            theirs, other_piece, own_piece = panel_product(known_inverse, arrays, places, band, col_index, False)
+        else:
+            theirs, mine, other_piece, own_piece = panel_product(
+                known_inverse, arrays, places, band, col_index, True
+            )
+            before = (products[-1][1], pieces[-1][1]) if products else ()
+            moving, theirs, other_piece, *before = lax.optimization_barrier((moving, theirs, other_piece, *before))
+            if before:
+                products[-1] = (products[-1][0], before[0], products[-1][2])
+                pieces[-1] = (pieces[-1][0], before[1], pieces[-1][2])
+        arrived = lax.ppermute(theirs, "col", pairs(2, 1))
+        arrived_piece = lax.ppermute(other_piece, ("row", "col"), to_other)
+        if last:
+            *arrays, crossed, crossed_piece = lax.optimization_barrier((*arrays, products[-1][1], pieces[-1][1]))
+            products[-1] = (products[-1][0], crossed, products[-1][2])
+            pieces[-1] = (pieces[-1][0], crossed_piece, pieces[-1][2])
+            mine, _, _ = panel_product(known_inverse, arrays, places, band, 1 - col_index, False)
+        products.append((mine, arrived, sources))
+        pieces.append((own_piece, arrived_piece, sources))
+
+    blocks_out = fold(products[-1:], matrix, fold(products[:-1], matrix, None))
+    first_block, second_block = blocks_out[:, :total], blocks_out[:, total:]
+    rows_one, rows_two = own_rows(pieces, (col_index == owner).astype(jnp.int32), total)
+    rows_two = rows_two - near(coupling, rows_one, (((0,), (0,)), ((), ())))
+    sums = (-near(rows_one, first_block), -near(rows_one, second_block), -near(rows_two, second_block))
+    bits = []
+    bit = 2
+    while bit < rows:
+        bits.append(("row", bit))
+        bit *= 2
+    ways = [("col", 1)] + bits
+    sums = [
+        summed(value, [("row", 1)] + ways[turn % len(ways) :] + ways[: turn % len(ways)])
+        for turn, value in enumerate(sums)
+    ]
+    col_width = total // 2
+
+    def own_columns(value):
+        return lax.dynamic_slice_in_dim(value, col_index * col_width, col_width, 1)
+
+    moved = near(first_diag, own_columns(coupling))
+    first_out = own_columns(first_diag) + sums[0]
+    cross_out = sums[1] - moved
+    second_out = own_columns(second_diag) + near(coupling, moved, (((0,), (0,)), ((), ()))) + sums[2]
+    return first_block, first_out, second_block, cross_out, second_out
+
+
+def on_device(*args):
+    known_inverse, first_panel, second_panel, coupling = args[:4]
+    first_present, second_present = args[6:]
+    rows, cols = lax.axis_size("row"), lax.axis_size("col")
+    band_rows, block_cols = known_inverse.shape
+    width = first_panel.shape[1]
+    fits = (
+        cols == 2
+        and rows >= 4
+        and rows & (rows - 1) == 0
+        and band_rows % (2 * BLK) == 0
+        and block_cols % (band_rows) == 0
+        and block_cols % (GROUP * BLK) == 0
+        and width % 32 == 0
+        and coupling.shape[0] % (2 * 16 * rows) == 0
+    )
+    if not fits:
+        return dense(*args)
+    blocks = block_cols // BLK
+    counts = (first_present + second_present).reshape(cols, blocks).sum(axis=1)
+    capacities = [int(share * 2 * blocks) for share in LEVELS]
+    level = sum((jnp.max(counts) > capacity).astype(jnp.int32) for capacity in capacities[:-1])
+    branches = [functools.partial(sparse, capacity=capacity) for capacity in capacities]
+    return lax.switch(level, branches, *args)
+
+
 def solution(mesh):
     in_specs = (P("row", "col"), P("col", "row"), P("col", "row"), P(), P(), P(), P(), P())
     out_specs = (

time: 557 us -> 327 us (0.59)
  waiting for transfers between devices: 312 us -> 44.3 us
  matrix products: 203 us -> 11.2 us
  Pallas kernels: 0 us -> 157 us
  starting transfers between devices: 0.69 us -> 60.5 us
  loops' own time: 0 us -> 18.5 us
  between operations: 14.3 us -> 3.04 us
  local copies, waits for them, and re-layouts: 10.3 us -> 17 us
    dot_general x8 -> x6, matrix products: 203 us -> 11.2 us  [near(): lax.dot_general(left, right, dims, precision=lax.Precision.HIGH, preferre...]
    pallas_call x0 -> x10, Pallas kernels: none -> 157 us  [the longest x6 136 us: panel_product(): pl.pallas_call(kernel, in_specs=[in_smem()] * 7 + [anywhere] * (1 + count...]
    psum x1 -> x0, waiting for transfers between devices: 132 us -> none  [on_device(): first_sum = lax.psum(first_partial, ('row', 'col'))]
    all_gather x2 -> x0, waiting for transfers between devices: 126 us -> none  [the longest x1 109 us: on_device(): lax.all_gather(local_one, 'row', axis=1, tiled=True)]
    ppermute x0 -> x46, starting transfers between devices: none -> 60.5 us  [the longest x15 17.2 us: summed(): value = mine + lax.ppermute(theirs, axis, pairs(count, bit))]
    reduce_scatter x4 -> x0, waiting for transfers between devices: 54 us -> none  [the longest x1 34.9 us: piece_products(): lax.psum_scatter(product(known_inverse, column_two), 'col', scatter_dimen...]
    ppermute x0 -> x46, waiting for transfers between devices: none -> 44.3 us  [the longest x4 14.4 us: sparse(): moving = lax.ppermute(moving, 'row', ring)]
    another operation x0 -> x1, loops' own time: none -> 18.5 us  [on_device(): return lax.switch(level, branches, *args)]
  transfers between devices with their start and end apart: 7 -> 46, of which waited for: 5 -> 15; matrix products, arithmetic and copies ran while one was open for 37% -> 5% of each run, Pallas kernels for 0% -> 45%
where the time goes in v1:
time: 327 us; the launch traced here: 326 us
  Pallas kernels  157 us (48%)
  starting transfers between devices  60.5 us (19%)
  waiting for transfers between devices  44.3 us (14%)
  loops' own time  18.5 us (6%)
  local copies, waits for them, and re-layouts  17 us (5%)
  other arithmetic  13.8 us (4%)
  matrix products  11.2 us (3%)
    pallas_call x6, Pallas kernels, panel_product(): pl.pallas_call(kernel, in_specs=[in_smem()] * 7 + [anywhere] * (1 + count...  136 us
    another operation x1, loops' own time, on_device(): return lax.switch(level, branches, *args)  18.5 us
    ppermute x15, starting transfers between devices, summed(): value = mine + lax.ppermute(theirs, axis, pairs(count, bit))  17.2 us
    ppermute x4, waiting for transfers between devices, sparse(): moving = lax.ppermute(moving, 'row', ring)  14.4 us
    cond x84, local copies, waits for them, and re-layouts  13.3 us
    ppermute x15, waiting for transfers between devices, summed(): value = mine + lax.ppermute(theirs, axis, pairs(count, bit))  13 us
    pallas_call x2, Pallas kernels, fold(): pl.pallas_call(kernel, in_specs=[in_smem()] + [in_vmem()] * (count + 1 +...  12.6 us
    ppermute x5, starting transfers between devices, sparse(): arrived = lax.ppermute(theirs, 'col', pairs(2, 1))  11.9 us
  transfers between devices with their start and end apart: 46, of which 15 were waited for; matrix products, arithmetic and copies ran while one was open for 5% of the time, Pallas kernels for 45%

profile of v1, /device:TPU:0, one launch (start us, length us, event | category | flops | bytes accessed | tf_op | source)
XLA Modules:
  0.0 325.5 jit_solution(6081166290196129284)
XLA Ops:
  3.5 321.0 %conditional.1 = (f32[640,512]{1,0:T(8,128)}, f32[512,256]{1,0:T(8,128)}, f32[640,512]{1,0:T(8,128)}, f32[512,256]{1,0:T(8,128)}, f32[512,256]{1,0:T(8,128)}) conditional(s32[]{:T(128)} %clamp.3, (s32[160]{0:T(256)}, s32[160]{0:T(256)}, f32[10240,32]{0,1:T(8,128)}, f32[10240,32]{0,1:T(8,128)}, f32[1280,10240]{1,0:T(8,128)}, ...), branch_computations={%region_2.0_spmd, %region_3.4_spmd, %region_4.5_spmd} | conditional | flops 89403187200 | bytes 605985088 | solution.py:563
  13.3 4.8 %present_rows.4 = (f32[32,12288]{1,0:T(8,128)S(1)}, s32[80]{0:T(128)S(1)}, s32[80]{0:T(128)S(1)}, s32[80]{0:T(128)S(1)}, s32[80]{0:T(128)S(1)}, /*index=5*/s32[80]{0:T(128)S(1)}, s32[1]{0:T(128)}) custom-call(s32[80]{0:T(128)S(1)} %dynamic_slice.245.one_ref, s32[80]{0:T(128)S(1)} %dynamic_slice.246.two_ref, f32[32,10240]{1,0:T(8,128)} %bitcast.106, ...), custom_call_target="tpu_custom_call" | custom-call | bytes 20971520 | tf_op jit(solution)/shard_map/cond/branch_1_fun/present_rows/pallas_call | solution.py:164
  18.6 3.2 collective-permute-done.46
  21.8 4.0 %maximum_select_fusion.13.refs_0_ = f32[64,12288]{1,0:T(8,128)} fusion(f32[32,12288]{1,0:T(8,128)} %collective-permute-done.46, f32[32,12288]{1,0:T(8,128)S(1)} %get-tuple-element.118, pred[]{:T(512)S(6)} %eq.168), kind=kLoop, calls=%fused_computation.66 | loop fusion | flops 2359296 | bytes 6291457 | tf_op jit(solution)/shard_map/cond/branch_1_fun/jit(_where)/select_n | solution.py:475
  25.8 2.9 collective-permute-start.47
  28.8 20.9 %panel_product.24 = (f32[640,128]{1,0:T(8,128)S(1)}, f32[640,128]{1,0:T(8,128)S(1)}, f32[128,640]{1,0:T(8,128)S(1)}, f32[128,640]{1,0:T(8,128)S(1)}) custom-call(s32[2]{0:T(128)S(1)} %pad_add_fusion.5.where_ref, s32[1]{0:T(128)} %get-tuple-element.111.size_ref, s32[80]{0:T(128)S(1)} %get-tuple-element.112.list_ref, s32[80]{0:T(128)S(1)} %get-tuple-element.113.one_ref, ...), custom_call_target="tpu_custom_call" | custom-call | flops 10066329600 | bytes 39321600 | tf_op jit(solution)/shard_map/cond/branch_1_fun/panel_product/pallas_call | solution.py:278
  51.2 13.1 %collective-permute-done.47.refs_0_ = f32[64,12288]{1,0:T(8,128)} collective-permute-done((f32[64,12288]{1,0:T(8,128)}, f32[64,12288]{1,0:T(8,128)}, u32[]{:S(2)}, u32[]{:S(2)}) %collective-permute-start.47) | collective-permute-done | bytes 3145760 | tf_op jit(solution)/shard_map/cond/branch_1_fun/ppermute | solution.py:490
  64.2 2.1 collective-permute-start.48
  66.3 1.5 collective-permute-start.50
  67.8 2.5 collective-permute-start.51
  70.3 1.8 copy-done.119
  72.0 28.9 %panel_product.25 = (f32[640,256]{1,0:T(8,128)S(1)}, f32[640,256]{1,0:T(8,128)S(1)}, f32[256,640]{1,0:T(8,128)S(1)}, f32[256,640]{1,0:T(8,128)S(1)}) custom-call(s32[2]{0:T(128)S(1)} %pad_add_fusion.5.where_ref, s32[1]{0:T(128)} %get-tuple-element.111.size_ref, s32[80]{0:T(128)S(1)} %get-tuple-element.112.list_ref, s32[80]{0:T(128)S(1)} %get-tuple-element.113.one_ref, ...), custom_call_target="tpu_custom_call" | custom-call | flops 20132659200 | bytes 39321600 | tf_op jit(solution)/shard_map/cond/branch_1_fun/panel_product/pallas_call | solution.py:278
  102.6 2.0 collective-permute-start.52
  104.6 2.9 collective-permute-start.54
  107.5 1.9 collective-permute-start.55
  110.1 28.7 %panel_product.26 = (f32[640,256]{1,0:T(8,128)S(1)}, f32[640,256]{1,0:T(8,128)S(1)}, f32[256,640]{1,0:T(8,128)S(1)}, f32[256,640]{1,0:T(8,128)S(1)}) custom-call(s32[2]{0:T(128)S(1)} %pad_add_fusion.5.where_ref, s32[1]{0:T(128)} %get-tuple-element.111.size_ref, s32[80]{0:T(128)S(1)} %get-tuple-element.112.list_ref, s32[80]{0:T(128)S(1)} %get-tuple-element.113.one_ref, ...), custom_call_target="tpu_custom_call" | custom-call | flops 20132659200 | bytes 39321600 | tf_op jit(solution)/shard_map/cond/branch_1_fun/panel_product/pallas_call | solution.py:278
  138.8 1.3 collective-permute-done.52.refs_0_
  140.3 1.5 copy-done.108
  141.8 1.9 collective-permute-start.56
  143.8 2.9 collective-permute-start.58
  146.7 1.9 collective-permute-start.59
  148.6 28.7 %panel_product.27 = (f32[640,256]{1,0:T(8,128)S(1)}, f32[640,256]{1,0:T(8,128)S(1)}, f32[256,640]{1,0:T(8,128)S(1)}, f32[256,640]{1,0:T(8,128)S(1)}) custom-call(s32[2]{0:T(128)S(1)} %pad_add_fusion.5.where_ref, s32[1]{0:T(128)} %get-tuple-element.111.size_ref, s32[80]{0:T(128)S(1)} %get-tuple-element.112.list_ref, s32[80]{0:T(128)S(1)} %get-tuple-element.113.one_ref, ...), custom_call_target="tpu_custom_call" | custom-call | flops 20132659200 | bytes 39321600 | tf_op jit(solution)/shard_map/cond/branch_1_fun/panel_product/pallas_call | solution.py:278
  184.0 2.2 collective-permute-start.61
  186.2 2.0 collective-permute-start.62
  188.2 2.5 select_maximum_fusion.1.refs_8_.refs_2_
  190.7 14.0 %panel_product.29 = (f32[640,128]{1,0:T(8,128)S(1)}, f32[128,640]{1,0:T(8,128)S(1)}, f32[128,640]{1,0:T(8,128)S(1)}) custom-call(s32[2]{0:T(128)S(1)} %copy-done.39, s32[1]{0:T(128)} %get-tuple-element.111.size_ref, s32[80]{0:T(128)S(1)} %get-tuple-element.112.list_ref, s32[80]{0:T(128)S(1)} %get-tuple-element.113.one_ref, ...), custom_call_target="tpu_custom_call" | custom-call | flops 5033164800 | bytes 19660800 | tf_op jit(solution)/shard_map/cond/branch_1_fun/panel_product/pallas_call | solution.py:278
  204.7 1.9 collective-permute-start.64
  206.7 8.9 %collective-permute-done.62.refs_7_ = f32[256,640]{1,0:T(8,128)S(1)} collective-permute-done((f32[256,640]{1,0:T(8,128)}, f32[256,640]{1,0:T(8,128)S(1)}, u32[]{:S(2)}, u32[]{:S(2)}) %collective-permute-start.62) | collective-permute-done | bytes 655392 | tf_op jit(solution)/shard_map/cond/branch_1_fun/ppermute | solution.py:504
  215.7 2.4 collective-permute-start.63
  218.1 15.2 %panel_product.28 = (f32[640,128]{1,0:T(8,128)S(1)}, f32[128,640]{1,0:T(8,128)}, f32[128,640]{1,0:T(8,128)}) custom-call(s32[2]{0:T(128)S(1)} %pad_add_fusion.4.where_ref, s32[1]{0:T(128)} %get-tuple-element.111.size_ref, s32[80]{0:T(128)S(1)} %get-tuple-element.112.list_ref, s32[80]{0:T(128)S(1)} %get-tuple-element.113.one_ref, ...), custom_call_target="tpu_custom_call" | custom-call | flops 5033164800 | bytes 19660800 | tf_op jit(solution)/shard_map/cond/branch_1_fun/panel_product/pallas_call | solution.py:278
  233.5 8.4 %fold.8.refs_3_ = f32[640,1024]{1,0:T(8,128)} custom-call(s32[7]{0:T(128)S(1)} %copy-done.41, f32[640,128]{1,0:T(8,128)S(1)} %copy-done.63, f32[640,128]{1,0:T(8,128)S(1)} %copy-done.69, f32[640,256]{1,0:T(8,128)S(1)} %copy-done.75, f32[640,256]{1,0:T(8,128)S(1)} %copy-done.45, f32[640,256]{1,0:T(8,128)S(1)} %copy-done.81, f32[640,256]{1,0:T(8,128)S(1)} %copy-done.51, ...), custom_call_target="tpu_custom_call" | custom-call | flops 3523215360 | bytes 5242880 | tf_op jit(solution)/shard_map/cond/branch_1_fun/fold/pallas_call | solution.py:332
  241.9 3.2 own_rows.4
  245.1 3.0 convolution_bitcast_fusion.2
  248.1 4.2 %fold.9 = f32[640,1024]{1,0:T(8,128)S(1)} custom-call(s32[2]{0:T(128)S(1)} %pad_add_fusion.3.first_ref, f32[640,128]{1,0:T(8,128)S(1)} %get-tuple-element.141.refs_0_, f32[640,128]{1,0:T(8,128)S(1)} %collective-permute-done.63.refs_1_, f32[1024,1024]{1,0:T(8,128)} %select_maximum_fusion.1.refs_8_.refs_2_, f32[640,1024]{1,0:T(8,128)} %fold.8.refs_3_), custom_call_target="tpu_custom_call" | custom-call | flops 503316480 | bytes 5242880 | tf_op jit(solution)/shard_map/cond/branch_1_fun/fold/pallas_call | solution.py:332
  252.6 1.3 copy-done.106
  253.9 1.4 convolution_negate_fusion.4
  255.3 1.4 convolution_negate_fusion.3
  257.5 1.5 convolution_negate_fusion.5
  259.3 1.7 collective-permute-start.84
  261.1 1.6 collective-permute-start.75
  262.8 1.0 collective-permute-start.66
  263.8 4.2 %collective-permute-done.84 = f32[128,512]{1,0:T(8,128)S(1)} collective-permute-done((f32[128,512]{1,0:T(8,128)S(1)}, f32[128,512]{1,0:T(8,128)S(1)}, u32[]{:S(2)}, u32[]{:S(2)}) %collective-permute-start.84) | collective-permute-done | bytes 262176 | tf_op jit(solution)/shard_map/cond/branch_1_fun/ppermute | solution.py:398
  268.1 2.3 collective-permute-start.85
  270.5 1.6 collective-permute-start.76
  272.7 4.4 %collective-permute-done.85 = f32[64,512]{1,0:T(8,128)S(1)} collective-permute-done((f32[64,512]{1,0:T(8,128)S(1)}, f32[64,512]{1,0:T(8,128)S(1)}, u32[]{:S(2)}, u32[]{:S(2)}) %collective-permute-start.85) | collective-permute-done | bytes 131104 | tf_op jit(solution)/shard_map/cond/branch_1_fun/ppermute | solution.py:398
  277.1 2.0 collective-permute-start.86
  279.2 1.1 collective-permute-start.77
  280.4 3.0 collective-permute-start.68
  283.9 1.2 collective-permute-done.77
  285.8 0.9 collective-permute-start.69
  287.8 1.4 collective-permute-done.78
  290.7 1.5 collective-permute-start.70
  292.2 1.5 collective-permute-start.89
  293.7 0.9 collective-permute-done.79
  294.7 1.1 collective-permute-start.80
  295.8 2.1 collective-permute-start.71
  297.9 1.4 collective-permute-start.90
  299.3 1.1 collective-permute-done.71
  301.2 1.5 collective-permute-start.81
  303.0 2.5 collective-permute-done.72
  306.2 1.1 fusion.13
  307.6 1.1 maximum_select_fusion.18
  309.3 2.1 fusion.10
  311.4 2.8 fusion.12
  (187 shorter events, 23.8 us)
Async XLA Ops:
  18.1 52.2 %copy-start.31 = (s32[80]{0:T(128)}, s32[80]{0:T(128)S(1)}, u32[]{:S(2)}) copy-start(s32[80]{0:T(128)S(1)} %get-tuple-element.116.by_two_ref) | copy-start | bytes 964 | tf_op jit(solution)/shard_map/cond
  18.1 3.7 %collective-permute-start.46 = (f32[32,12288]{1,0:T(8,128)S(1)}, f32[32,12288]{1,0:T(8,128)}, u32[]{:S(2)}, u32[]{:S(2)}) collective-permute-start(f32[32,12288]{1,0:T(8,128)S(1)} %get-tuple-element.118), channel_id=1, source_target_pairs={{0,2},{2,0},{4,6},{6,4},{8,10},{10,8},{12,14},{14,12},{16,18},{18,... | collective-permute-start | bytes 4718600 | tf_op jit(solution)/shard_map/cond/branch_1_fun/ppermute | solution.py:460
  25.8 38.5 %collective-permute-start.47 = (f32[64,12288]{1,0:T(8,128)}, f32[64,12288]{1,0:T(8,128)}, u32[]{:S(2)}, u32[]{:S(2)}) collective-permute-start(f32[64,12288]{1,0:T(8,128)} %maximum_select_fusion.13.refs_0_), channel_id=1, source_target_pairs={{0,8},{2,6},{8,16},{10,2},{16,24},{18,10},{24,28},{26,18},{28,20},... | collective-permute-start | bytes 9437192 | tf_op jit(solution)/shard_map/cond/branch_1_fun/ppermute | solution.py:490
  28.8 119.8 %copy-start.38 = (s32[2]{0:T(128)}, s32[2]{0:T(128)S(1)}, u32[]{:S(2)}) copy-start(s32[2]{0:T(128)S(1)} %pad_add_fusion.5.where_ref) | copy-start | bytes 28 | tf_op jit(solution)/shard_map/cond
  64.2 6.0 %collective-permute-start.49 = (f32[64,12288]{1,0:T(8,128)}, f32[64,12288]{1,0:T(8,128)S(1)}, u32[]{:S(2)}, u32[]{:S(2)}) collective-permute-start(f32[64,12288]{1,0:T(8,128)} %collective-permute-done.47.refs_0_), channel_id=1, source_target_pairs={{0,2},{2,0},{4,6},{6,4},{8,10},{10,8},{12,14},{14,12},{16,18},{18,... | collective-permute-start | bytes 9437192 | tf_op jit(solution)/shard_map/cond/branch_1_fun/ppermute | solution.py:460
  64.2 38.3 %collective-permute-start.48 = (f32[64,12288]{1,0:T(8,128)}, f32[64,12288]{1,0:T(8,128)}, u32[]{:S(2)}, u32[]{:S(2)}) collective-permute-start(f32[64,12288]{1,0:T(8,128)} %collective-permute-done.47.refs_0_), channel_id=1, source_target_pairs={{0,8},{2,6},{8,16},{10,2},{16,24},{18,10},{24,28},{26,18},{28,20},... | collective-permute-start | bytes 9437192 | tf_op jit(solution)/shard_map/cond/branch_1_fun/ppermute | solution.py:490
  66.3 35.5 %collective-permute-start.50 = (f32[640,128]{1,0:T(8,128)S(1)}, f32[640,128]{1,0:T(8,128)S(1)}, u32[]{:S(2)}, u32[]{:S(2)}) collective-permute-start(f32[640,128]{1,0:T(8,128)S(1)} %get-tuple-element.124), channel_id=1, source_target_pairs={{0,1},{1,0},{2,3},{3,2},{4,5},{5,4},{6,7},{7,6},{8,9},{9,8},{10,11... | collective-permute-start | bytes 983048 | tf_op jit(solution)/shard_map/cond/branch_1_fun/ppermute | solution.py:503
  67.8 34.7 %collective-permute-start.51 = (f32[128,640]{1,0:T(8,128)S(1)}, f32[128,640]{1,0:T(8,128)S(1)}, u32[]{:S(2)}, u32[]{:S(2)}) collective-permute-start(f32[128,640]{1,0:T(8,128)S(1)} %get-tuple-element.125), channel_id=1, source_target_pairs={{0,1},{2,3},{4,5},{6,7},{8,9},{10,11},{12,13},{14,15},{17,16},{19,... | collective-permute-start | bytes 983048 | tf_op jit(solution)/shard_map/cond/branch_1_fun/ppermute | solution.py:504
  102.5 36.3 %copy-start.25 = (f32[128,640]{1,0:T(8,128)}, f32[128,640]{1,0:T(8,128)S(1)}, u32[]{:S(2)}) copy-start(f32[128,640]{1,0:T(8,128)S(1)} %collective-permute-done.51.refs_1_) | copy-start | bytes 983044 | tf_op jit(solution)/shard_map/cond
  102.5 7.0 %collective-permute-start.53 = (f32[64,12288]{1,0:T(8,128)}, f32[64,12288]{1,0:T(8,128)}, u32[]{:S(2)}, u32[]{:S(2)}) collective-permute-start(f32[64,12288]{1,0:T(8,128)} %collective-permute-done.48.refs_0_), channel_id=1, source_target_pairs={{0,2},{2,0},{4,6},{6,4},{8,10},{10,8},{12,14},{14,12},{16,18},{18,... | collective-permute-start | bytes 9437192 | tf_op jit(solution)/shard_map/cond/branch_1_fun/ppermute | solution.py:460
  102.6 37.5 %collective-permute-start.52 = (f32[64,12288]{1,0:T(8,128)}, f32[64,12288]{1,0:T(8,128)S(1)}, u32[]{:S(2)}, u32[]{:S(2)}) collective-permute-start(f32[64,12288]{1,0:T(8,128)} %collective-permute-done.48.refs_0_), channel_id=1, source_target_pairs={{0,8},{2,6},{8,16},{10,2},{16,24},{18,10},{24,28},{26,18},{28,20},... | collective-permute-start | bytes 9437192 | tf_op jit(solution)/shard_map/cond/branch_1_fun/ppermute | solution.py:490
  104.6 34.2 %collective-permute-start.54 = (f32[640,256]{1,0:T(8,128)S(1)}, f32[640,256]{1,0:T(8,128)S(1)}, u32[]{:S(2)}, u32[]{:S(2)}) collective-permute-start(f32[640,256]{1,0:T(8,128)S(1)} %get-tuple-element.129), channel_id=1, source_target_pairs={{0,1},{1,0},{2,3},{3,2},{4,5},{5,4},{6,7},{7,6},{8,9},{9,8},{10,11... | collective-permute-start | bytes 1966088 | tf_op jit(solution)/shard_map/cond/branch_1_fun/ppermute | solution.py:503
  107.5 31.3 %collective-permute-start.55 = (f32[256,640]{1,0:T(8,128)S(1)}, f32[256,640]{1,0:T(8,128)S(1)}, u32[]{:S(2)}, u32[]{:S(2)}) collective-permute-start(f32[256,640]{1,0:T(8,128)S(1)} %get-tuple-element.130), channel_id=1, source_target_pairs={{0,1},{2,3},{4,5},{6,7},{8,9},{10,11},{12,13},{14,15},{17,16},{19,... | collective-permute-start | bytes 1966088 | tf_op jit(solution)/shard_map/cond/branch_1_fun/ppermute | solution.py:504
  140.1 8.5 %collective-permute-start.57 = (f32[64,12288]{1,0:T(8,128)S(1)}, f32[64,12288]{1,0:T(8,128)}, u32[]{:S(2)}, u32[]{:S(2)}) collective-permute-start(f32[64,12288]{1,0:T(8,128)S(1)} %collective-permute-done.52.refs_0_), channel_id=1, source_target_pairs={{0,2},{2,0},{4,6},{6,4},{8,10},{10,8},{12,14},{14,12},{16,18},{18,... | collective-permute-start | bytes 9437192 | tf_op jit(solution)/shard_map/cond/branch_1_fun/ppermute | solution.py:460
  141.8 40.7 %collective-permute-start.56 = (f32[32,12288]{1,0:T(8,128)S(1)}, f32[32,12288]{1,0:T(8,128)S(1)}, u32[]{:S(2)}, u32[]{:S(2)}) collective-permute-start(f32[32,12288]{1,0:T(8,128)S(1)} %slice_select_fusion.1), channel_id=1, source_target_pairs={{0,8},{2,6},{8,16},{10,2},{16,24},{18,10},{24,28},{26,18},{28,20},... | collective-permute-start | bytes 4718600 | tf_op jit(solution)/shard_map/cond/branch_1_fun/ppermute | solution.py:490
  143.8 36.9 %collective-permute-start.58 = (f32[640,256]{1,0:T(8,128)S(1)}, f32[640,256]{1,0:T(8,128)S(1)}, u32[]{:S(2)}, u32[]{:S(2)}) collective-permute-start(f32[640,256]{1,0:T(8,128)S(1)} %get-tuple-element.134), channel_id=1, source_target_pairs={{0,1},{1,0},{2,3},{3,2},{4,5},{5,4},{6,7},{7,6},{8,9},{9,8},{10,11... | collective-permute-start | bytes 1966088 | tf_op jit(solution)/shard_map/cond/branch_1_fun/ppermute | solution.py:503
  146.7 34.9 %collective-permute-start.59 = (f32[256,640]{1,0:T(8,128)S(1)}, f32[256,640]{1,0:T(8,128)S(1)}, u32[]{:S(2)}, u32[]{:S(2)}) collective-permute-start(f32[256,640]{1,0:T(8,128)S(1)} %get-tuple-element.135), channel_id=1, source_target_pairs={{0,1},{2,3},{4,5},{6,7},{8,9},{10,11},{12,13},{14,15},{17,16},{19,... | collective-permute-start | bytes 1966088 | tf_op jit(solution)/shard_map/cond/branch_1_fun/ppermute | solution.py:504
  182.5 8.3 %collective-permute-start.60 = (f32[32,12288]{1,0:T(8,128)S(1)}, f32[32,12288]{1,0:T(8,128)}, u32[]{:S(2)}, u32[]{:S(2)}) collective-permute-start(f32[32,12288]{1,0:T(8,128)S(1)} %collective-permute-done.56.refs_0_), channel_id=1, source_target_pairs={{0,2},{2,0},{4,6},{6,4},{8,10},{10,8},{12,14},{14,12},{16,18},{18,... | collective-permute-start | bytes 4718600 | tf_op jit(solution)/shard_map/cond/branch_1_fun/ppermute | solution.py:460
  184.0 22.6 %collective-permute-start.61 = (f32[640,256]{1,0:T(8,128)}, f32[640,256]{1,0:T(8,128)S(1)}, u32[]{:S(2)}, u32[]{:S(2)}) collective-permute-start(f32[640,256]{1,0:T(8,128)} %copy-done.58), channel_id=1, source_target_pairs={{0,1},{1,0},{2,3},{3,2},{4,5},{5,4},{6,7},{7,6},{8,9},{9,8},{10,11... | collective-permute-start | bytes 1966088 | tf_op jit(solution)/shard_map/cond/branch_1_fun/ppermute | solution.py:503
  186.2 29.4 %collective-permute-start.62 = (f32[256,640]{1,0:T(8,128)}, f32[256,640]{1,0:T(8,128)S(1)}, u32[]{:S(2)}, u32[]{:S(2)}) collective-permute-start(f32[256,640]{1,0:T(8,128)} %copy-done.55), channel_id=1, source_target_pairs={{0,1},{2,3},{4,5},{6,7},{8,9},{10,11},{12,13},{14,15},{17,16},{19,... | collective-permute-start | bytes 1966088 | tf_op jit(solution)/shard_map/cond/branch_1_fun/ppermute | solution.py:504
  204.7 37.2 %collective-permute-start.64 = (f32[128,640]{1,0:T(8,128)S(1)}, f32[128,640]{1,0:T(8,128)S(1)}, u32[]{:S(2)}, u32[]{:S(2)}) collective-permute-start(f32[128,640]{1,0:T(8,128)S(1)} %get-tuple-element.162), channel_id=1, source_target_pairs={{0,1},{2,3},{4,5},{6,7},{8,9},{10,11},{12,13},{14,15},{17,16},{19,... | collective-permute-start | bytes 983048 | tf_op jit(solution)/shard_map/cond/branch_1_fun/ppermute | solution.py:504
  206.7 26.7 %copy-start.123 = (f32[640,256]{1,0:T(8,128)}, f32[640,256]{1,0:T(8,128)S(1)}, u32[]{:S(2)}) copy-start(f32[640,256]{1,0:T(8,128)S(1)} %collective-permute-done.61.refs_7_) | copy-start | bytes 1966084 | tf_op jit(solution)/shard_map/cond
  215.6 17.8 %copy-start.117 = (f32[256,640]{1,0:T(8,128)}, f32[256,640]{1,0:T(8,128)S(1)}, u32[]{:S(2)}) copy-start(f32[256,640]{1,0:T(8,128)S(1)} %collective-permute-done.62.refs_7_) | copy-start | bytes 1966084 | tf_op jit(solution)/shard_map/cond
  215.6 17.8 %copy-start.41 = (s32[7]{0:T(128)S(1)}, s32[7]{0:T(128)}, u32[]{:S(2)}) copy-start(s32[7]{0:T(128)} %stack.174.first_ref) | copy-start | bytes 88 | tf_op jit(solution)/shard_map/cond
  215.6 17.8 %copy-start.45 = (f32[640,256]{1,0:T(8,128)S(1)}, f32[640,256]{1,0:T(8,128)}, u32[]{:S(2)}) copy-start(f32[640,256]{1,0:T(8,128)} %copy-done.44) | copy-start | bytes 1966084 | tf_op jit(solution)/shard_map/cond
  215.6 17.8 %copy-start.51 = (f32[640,256]{1,0:T(8,128)S(1)}, f32[640,256]{1,0:T(8,128)}, u32[]{:S(2)}) copy-start(f32[640,256]{1,0:T(8,128)} %copy-done.50) | copy-start | bytes 1966084 | tf_op jit(solution)/shard_map/cond
  215.6 17.8 %copy-start.63 = (f32[640,128]{1,0:T(8,128)S(1)}, f32[640,128]{1,0:T(8,128)}, u32[]{:S(2)}) copy-start(f32[640,128]{1,0:T(8,128)} %copy-done.62) | copy-start | bytes 983044 | tf_op jit(solution)/shard_map/cond
  215.6 17.8 %copy-start.69 = (f32[640,128]{1,0:T(8,128)S(1)}, f32[640,128]{1,0:T(8,128)}, u32[]{:S(2)}) copy-start(f32[640,128]{1,0:T(8,128)} %copy-done.68) | copy-start | bytes 983044 | tf_op jit(solution)/shard_map/cond
  215.6 17.8 %copy-start.75 = (f32[640,256]{1,0:T(8,128)S(1)}, f32[640,256]{1,0:T(8,128)}, u32[]{:S(2)}) copy-start(f32[640,256]{1,0:T(8,128)} %copy-done.74) | copy-start | bytes 1966084 | tf_op jit(solution)/shard_map/cond
  215.6 17.8 %copy-start.81 = (f32[640,256]{1,0:T(8,128)S(1)}, f32[640,256]{1,0:T(8,128)}, u32[]{:S(2)}) copy-start(f32[640,256]{1,0:T(8,128)} %copy-done.80) | copy-start | bytes 1966084 | tf_op jit(solution)/shard_map/cond
  215.7 17.8 %copy-start.87 = (f32[640,256]{1,0:T(8,128)S(1)}, f32[640,256]{1,0:T(8,128)}, u32[]{:S(2)}) copy-start(f32[640,256]{1,0:T(8,128)} %copy-done.86) | copy-start | bytes 1966084 | tf_op jit(solution)/shard_map/cond
  215.7 32.4 %collective-permute-start.63 = (f32[640,128]{1,0:T(8,128)S(1)}, f32[640,128]{1,0:T(8,128)S(1)}, u32[]{:S(2)}, u32[]{:S(2)}) collective-permute-start(f32[640,128]{1,0:T(8,128)S(1)} %get-tuple-element.142), channel_id=1, source_target_pairs={{0,1},{1,0},{2,3},{3,2},{4,5},{5,4},{6,7},{7,6},{8,9},{9,8},{10,11... | collective-permute-start | bytes 983048 | tf_op jit(solution)/shard_map/cond/branch_1_fun/ppermute | solution.py:503
  233.5 8.4 %copy-start.11 = (f32[256,640]{1,0:T(8,128)S(1)}, f32[256,640]{1,0:T(8,128)}, u32[]{:S(2)}) copy-start(f32[256,640]{1,0:T(8,128)} %copy-done.10) | copy-start | bytes 1966084 | tf_op jit(solution)/shard_map/cond
  233.5 8.4 %copy-start.20 = (f32[128,640]{1,0:T(8,128)S(1)}, f32[128,640]{1,0:T(8,128)}, u32[]{:S(2)}) copy-start(f32[128,640]{1,0:T(8,128)} %copy-done.19) | copy-start | bytes 983044 | tf_op jit(solution)/shard_map/cond
  233.5 8.4 %copy-start.26 = (f32[128,640]{1,0:T(8,128)S(1)}, f32[128,640]{1,0:T(8,128)}, u32[]{:S(2)}) copy-start(f32[128,640]{1,0:T(8,128)} %copy-done.25) | copy-start | bytes 983044 | tf_op jit(solution)/shard_map/cond
  233.5 8.4 %copy-start.37 = (s32[10]{0:T(128)S(1)}, s32[10]{0:T(128)}, u32[]{:S(2)}) copy-start(s32[10]{0:T(128)} %stack.177.first_ref) | copy-start | bytes 124 | tf_op jit(solution)/shard_map/cond
  256.8 2.3 collective-permute-start.83
  257.0 4.0 %collective-permute-start.74 = (f32[256,512]{1,0:T(8,128)S(1)}, f32[256,512]{1,0:T(8,128)S(1)}, u32[]{:S(2)}, u32[]{:S(2)}) collective-permute-start(f32[256,512]{1,0:T(8,128)S(1)} %constant_dynamic-slice_fusion.24), channel_id=1, source_target_pairs={{0,2},{2,0},{4,6},{6,4},{8,10},{10,8},{12,14},{14,12},{16,18},{18,... | collective-permute-start | bytes 1572872 | tf_op jit(solution)/shard_map/cond/branch_1_fun/ppermute | solution.py:398
  259.1 3.6 %collective-permute-start.65 = (f32[256,512]{1,0:T(8,128)S(1)}, f32[256,512]{1,0:T(8,128)S(1)}, u32[]{:S(2)}, u32[]{:S(2)}) collective-permute-start(f32[256,512]{1,0:T(8,128)S(1)} %constant_dynamic-slice_fusion.29), channel_id=1, source_target_pairs={{0,2},{2,0},{4,6},{6,4},{8,10},{10,8},{12,14},{14,12},{16,18},{18,... | collective-permute-start | bytes 1572872 | tf_op jit(solution)/shard_map/cond/branch_1_fun/ppermute | solution.py:398
  259.3 8.8 %collective-permute-start.84 = (f32[128,512]{1,0:T(8,128)S(1)}, f32[128,512]{1,0:T(8,128)S(1)}, u32[]{:S(2)}, u32[]{:S(2)}) collective-permute-start(f32[128,512]{1,0:T(8,128)S(1)} %constant_dynamic-slice_fusion.18), channel_id=1, source_target_pairs={{0,8},{2,10},{4,12},{6,14},{8,0},{10,2},{12,4},{14,6},{16,24},{18,... | collective-permute-start | bytes 786440 | tf_op jit(solution)/shard_map/cond/branch_1_fun/ppermute | solution.py:398
  261.1 9.4 %collective-permute-start.75 = (f32[128,512]{1,0:T(8,128)S(1)}, f32[128,512]{1,0:T(8,128)S(1)}, u32[]{:S(2)}, u32[]{:S(2)}) collective-permute-start(f32[128,512]{1,0:T(8,128)S(1)} %constant_dynamic-slice_fusion.23), channel_id=1, source_target_pairs={{0,4},{2,6},{4,0},{6,2},{8,12},{10,14},{12,8},{14,10},{16,20},{18,... | collective-permute-start | bytes 786440 | tf_op jit(solution)/shard_map/cond/branch_1_fun/ppermute | solution.py:398
  262.8 9.3 %collective-permute-start.66 = (f32[256,256]{1,0:T(8,128)S(1)}, f32[256,256]{1,0:T(8,128)S(1)}, u32[]{:S(2)}, u32[]{:S(2)}) collective-permute-start(f32[256,256]{1,0:T(8,128)S(1)} %constant_dynamic-slice_fusion.28), channel_id=1, source_target_pairs={{0,1},{1,0},{2,3},{3,2},{4,5},{5,4},{6,7},{7,6},{8,9},{9,8},{10,11... | collective-permute-start | bytes 786440 | tf_op jit(solution)/shard_map/cond/branch_1_fun/ppermute | solution.py:398
  268.1 9.0 %collective-permute-start.85 = (f32[64,512]{1,0:T(8,128)S(1)}, f32[64,512]{1,0:T(8,128)S(1)}, u32[]{:S(2)}, u32[]{:S(2)}) collective-permute-start(f32[64,512]{1,0:T(8,128)S(1)} %constant_dynamic-slice_fusion.17), channel_id=1, source_target_pairs={{0,16},{2,18},{4,20},{6,22},{8,24},{10,26},{12,28},{14,30},{16,0},... | collective-permute-start | bytes 393224 | tf_op jit(solution)/shard_map/cond/branch_1_fun/ppermute | solution.py:398
  270.5 8.7 %collective-permute-start.76 = (f32[64,512]{1,0:T(8,128)S(1)}, f32[64,512]{1,0:T(8,128)S(1)}, u32[]{:S(2)}, u32[]{:S(2)}) collective-permute-start(f32[64,512]{1,0:T(8,128)S(1)} %constant_dynamic-slice_fusion.22), channel_id=1, source_target_pairs={{0,8},{2,10},{4,12},{6,14},{8,0},{10,2},{12,4},{14,6},{16,24},{18,... | collective-permute-start | bytes 393224 | tf_op jit(solution)/shard_map/cond/branch_1_fun/ppermute | solution.py:398
  272.2 8.1 %collective-permute-start.67 = (f32[128,256]{1,0:T(8,128)S(1)}, f32[128,256]{1,0:T(8,128)S(1)}, u32[]{:S(2)}, u32[]{:S(2)}) collective-permute-start(f32[128,256]{1,0:T(8,128)S(1)} %constant_dynamic-slice_fusion.27), channel_id=1, source_target_pairs={{0,4},{2,6},{4,0},{6,2},{8,12},{10,14},{12,8},{14,10},{16,20},{18,... | collective-permute-start | bytes 393224 | tf_op jit(solution)/shard_map/cond/branch_1_fun/ppermute | solution.py:398
  277.1 6.3 %collective-permute-start.86 = (f32[64,256]{1,0:T(8,128)S(1)}, f32[64,256]{1,0:T(8,128)S(1)}, u32[]{:S(2)}, u32[]{:S(2)}) collective-permute-start(f32[64,256]{1,0:T(8,128)S(1)} %constant_dynamic-slice_fusion.16), channel_id=1, source_target_pairs={{0,1},{1,0},{2,3},{3,2},{4,5},{5,4},{6,7},{7,6},{8,9},{9,8},{10,11... | collective-permute-start | bytes 196616 | tf_op jit(solution)/shard_map/cond/branch_1_fun/ppermute | solution.py:398
  279.2 6.0 %collective-permute-start.77 = (f32[32,512]{1,0:T(8,128)S(1)}, f32[32,512]{1,0:T(8,128)S(1)}, u32[]{:S(2)}, u32[]{:S(2)}) collective-permute-start(f32[32,512]{1,0:T(8,128)S(1)} %constant_dynamic-slice_fusion.21), channel_id=1, source_target_pairs={{0,16},{2,18},{4,20},{6,22},{8,24},{10,26},{12,28},{14,30},{16,0},... | collective-permute-start | bytes 196616 | tf_op jit(solution)/shard_map/cond/branch_1_fun/ppermute | solution.py:398
  280.4 5.4 %collective-permute-start.68 = (f32[64,256]{1,0:T(8,128)S(1)}, f32[64,256]{1,0:T(8,128)S(1)}, u32[]{:S(2)}, u32[]{:S(2)}) collective-permute-start(f32[64,256]{1,0:T(8,128)S(1)} %constant_dynamic-slice_fusion.26), channel_id=1, source_target_pairs={{0,8},{2,10},{4,12},{6,14},{8,0},{10,2},{12,4},{14,6},{16,24},{18,... | collective-permute-start | bytes 196616 | tf_op jit(solution)/shard_map/cond/branch_1_fun/ppermute | solution.py:398
  283.4 4.0 %collective-permute-start.87 = (f32[32,256]{1,0:T(8,128)S(1)}, f32[32,256]{1,0:T(8,128)S(1)}, u32[]{:S(2)}, u32[]{:S(2)}) collective-permute-start(f32[32,256]{1,0:T(8,128)S(1)} %constant_dynamic-slice_fusion.15), channel_id=1, source_target_pairs={{0,4},{2,6},{4,0},{6,2},{8,12},{10,14},{12,8},{14,10},{16,20},{18,... | collective-permute-start | bytes 98312 | tf_op jit(solution)/shard_map/cond/branch_1_fun/ppermute | solution.py:398
  285.2 21.1 %copy-start.100 = (f32[512,512]{1,0:T(8,128)S(1)}, f32[512,512]{1,0:T(8,128)}, u32[]{:S(2)}) copy-start(f32[512,512]{1,0:T(8,128)} %get-tuple-element.152) | copy-start | bytes 3145732 | tf_op jit(solution)/shard_map/cond
  285.2 4.0 %collective-permute-start.78 = (f32[32,256]{1,0:T(8,128)S(1)}, f32[32,256]{1,0:T(8,128)S(1)}, u32[]{:S(2)}, u32[]{:S(2)}) collective-permute-start(f32[32,256]{1,0:T(8,128)S(1)} %constant_dynamic-slice_fusion.20), channel_id=1, source_target_pairs={{0,1},{1,0},{2,3},{3,2},{4,5},{5,4},{6,7},{7,6},{8,9},{9,8},{10,11... | collective-permute-start | bytes 98312 | tf_op jit(solution)/shard_map/cond/branch_1_fun/ppermute | solution.py:398
  285.8 4.9 %collective-permute-start.69 = (f32[32,256]{1,0:T(8,128)S(1)}, f32[32,256]{1,0:T(8,128)S(1)}, u32[]{:S(2)}, u32[]{:S(2)}) collective-permute-start(f32[32,256]{1,0:T(8,128)S(1)} %constant_dynamic-slice_fusion.25), channel_id=1, source_target_pairs={{0,16},{2,18},{4,20},{6,22},{8,24},{10,26},{12,28},{14,30},{16,0},... | collective-permute-start | bytes 98312 | tf_op jit(solution)/shard_map/cond/branch_1_fun/ppermute | solution.py:398
  287.4 4.8 %collective-permute-start.88 = (f32[32,256]{1,0:T(8,128)S(1)}, f32[32,256]{1,0:T(8,128)S(1)}, u32[]{:S(2)}, u32[]{:S(2)}) collective-permute-start(f32[32,256]{1,0:T(8,128)S(1)} %dynamic-slice_add_fusion.27), channel_id=1, source_target_pairs={{0,4},{2,6},{4,0},{6,2},{8,12},{10,14},{12,8},{14,10},{16,20},{18,... | collective-permute-start | bytes 98312 | tf_op jit(solution)/shard_map/cond/branch_1_fun/ppermute | solution.py:402
  289.2 5.5 %collective-permute-start.79 = (f32[32,256]{1,0:T(8,128)S(1)}, f32[32,256]{1,0:T(8,128)S(1)}, u32[]{:S(2)}, u32[]{:S(2)}) collective-permute-start(f32[32,256]{1,0:T(8,128)S(1)} %dynamic-slice_add_fusion.28), channel_id=1, source_target_pairs={{0,16},{2,18},{4,20},{6,22},{8,24},{10,26},{12,28},{14,30},{16,0},... | collective-permute-start | bytes 98312 | tf_op jit(solution)/shard_map/cond/branch_1_fun/ppermute | solution.py:402
  290.7 5.1 %collective-permute-start.70 = (f32[32,256]{1,0:T(8,128)S(1)}, f32[32,256]{1,0:T(8,128)S(1)}, u32[]{:S(2)}, u32[]{:S(2)}) collective-permute-start(f32[32,256]{1,0:T(8,128)S(1)} %dynamic-slice_add_fusion.29), channel_id=1, source_target_pairs={{0,16},{2,18},{4,20},{6,22},{8,24},{10,26},{12,28},{14,30},{16,0},... | collective-permute-start | bytes 98312 | tf_op jit(solution)/shard_map/cond/branch_1_fun/ppermute | solution.py:402
  292.2 5.7 %collective-permute-start.89 = (f32[64,256]{1,0:T(8,128)S(1)}, f32[64,256]{1,0:T(8,128)S(1)}, u32[]{:S(2)}, u32[]{:S(2)}) collective-permute-start(f32[64,256]{1,0:T(8,128)S(1)} %maximum_select_fusion.25), channel_id=1, source_target_pairs={{0,16},{2,18},{4,20},{6,22},{8,24},{10,26},{12,28},{14,30},{16,0},... | collective-permute-start | bytes 196616 | tf_op jit(solution)/shard_map/cond/branch_1_fun/ppermute | solution.py:402
  294.7 6.5 %collective-permute-start.80 = (f32[64,256]{1,0:T(8,128)S(1)}, f32[64,256]{1,0:T(8,128)S(1)}, u32[]{:S(2)}, u32[]{:S(2)}) collective-permute-start(f32[64,256]{1,0:T(8,128)S(1)} %maximum_select_fusion.24), channel_id=1, source_target_pairs={{0,8},{2,10},{4,12},{6,14},{8,0},{10,2},{12,4},{14,6},{16,24},{18,... | collective-permute-start | bytes 196616 | tf_op jit(solution)/shard_map/cond/branch_1_fun/ppermute | solution.py:402
  295.8 4.6 %collective-permute-start.71 = (f32[64,256]{1,0:T(8,128)S(1)}, f32[64,256]{1,0:T(8,128)S(1)}, u32[]{:S(2)}, u32[]{:S(2)}) collective-permute-start(f32[64,256]{1,0:T(8,128)S(1)} %maximum_select_fusion.23), channel_id=1, source_target_pairs={{0,8},{2,10},{4,12},{6,14},{8,0},{10,2},{12,4},{14,6},{16,24},{18,... | collective-permute-start | bytes 196616 | tf_op jit(solution)/shard_map/cond/branch_1_fun/ppermute | solution.py:402
  297.9 5.0 %collective-permute-start.90 = (f32[128,256]{1,0:T(8,128)S(1)}, f32[128,256]{1,0:T(8,128)S(1)}, u32[]{:S(2)}, u32[]{:S(2)}) collective-permute-start(f32[128,256]{1,0:T(8,128)S(1)} %maximum_select_fusion.22), channel_id=1, source_target_pairs={{0,8},{2,10},{4,12},{6,14},{8,0},{10,2},{12,4},{14,6},{16,24},{18,... | collective-permute-start | bytes 393224 | tf_op jit(solution)/shard_map/cond/branch_1_fun/ppermute | solution.py:402
  300.5 5.0 %collective-permute-start.72 = (f32[128,256]{1,0:T(8,128)S(1)}, f32[128,256]{1,0:T(8,128)S(1)}, u32[]{:S(2)}, u32[]{:S(2)}) collective-permute-start(f32[128,256]{1,0:T(8,128)S(1)} %maximum_select_fusion.20), channel_id=1, source_target_pairs={{0,4},{2,6},{4,0},{6,2},{8,12},{10,14},{12,8},{14,10},{16,20},{18,... | collective-permute-start | bytes 393224 | tf_op jit(solution)/shard_map/cond/branch_1_fun/ppermute | solution.py:402
  301.2 6.4 %collective-permute-start.81 = (f32[128,256]{1,0:T(8,128)S(1)}, f32[128,256]{1,0:T(8,128)}, u32[]{:S(2)}, u32[]{:S(2)}) collective-permute-start(f32[128,256]{1,0:T(8,128)S(1)} %maximum_select_fusion.21), channel_id=1, source_target_pairs={{0,4},{2,6},{4,0},{6,2},{8,12},{10,14},{12,8},{14,10},{16,20},{18,... | collective-permute-start | bytes 393224 | tf_op jit(solution)/shard_map/cond/branch_1_fun/ppermute | solution.py:402
  303.0 8.4 %collective-permute-start.91 = (f32[256,256]{1,0:T(8,128)S(1)}, f32[256,256]{1,0:T(8,128)}, u32[]{:S(2)}, u32[]{:S(2)}) collective-permute-start(f32[256,256]{1,0:T(8,128)S(1)} %maximum_select_fusion.19), channel_id=1, source_target_pairs={{0,2},{2,0},{4,6},{6,4},{8,10},{10,8},{12,14},{14,12},{16,18},{18,... | collective-permute-start | bytes 786440 | tf_op jit(solution)/shard_map/cond/branch_1_fun/ppermute | solution.py:402
  306.2 3.0 collective-permute-start.73
  308.7 5.5 %collective-permute-start.82 = (f32[256,256]{1,0:T(8,128)S(1)}, f32[256,256]{1,0:T(8,128)S(1)}, u32[]{:S(2)}, u32[]{:S(2)}) collective-permute-start(f32[256,256]{1,0:T(8,128)S(1)} %maximum_select_fusion.18), channel_id=1, source_target_pairs={{0,2},{2,0},{4,6},{6,4},{8,10},{10,8},{12,14},{14,12},{16,18},{18,... | collective-permute-start | bytes 786440 | tf_op jit(solution)/shard_map/cond/branch_1_fun/ppermute | solution.py:402
  (24 other events, 43.3 us)
